TPU v7x, 256 devices: a whole 4x4x8 slice. The times are simulated.
256 devices in a mesh: pos: 64 (over x, z, core), kvh: 4 (over y).
Axes of the slice: x: 4, y: 4, z: 8, core: 2. Of those that a mesh axis runs over, the one named last changes fastest.
Arguments:
- queries: bfloat16 [256, 64, 128], P('pos', 'kvh'), may hold values from -112 to 112
- prefix_keys: bfloat16 [262144, 8, 128], P('pos', 'kvh'), may hold values from -4 to 4
- prefix_values: bfloat16 [262144, 8, 128], P('pos', 'kvh'), may hold values from -6 to 6
- suffix_keys: bfloat16 [256, 1024, 8, 128], P('pos', None, 'kvh'), may hold values from -6 to 6
- suffix_values: bfloat16 [256, 1024, 8, 128], P('pos', None, 'kvh'), may hold values from -6 to 6
- suffix_lengths: int32 [256], P('pos'), may hold values from 1 to 1024, as said below
Outputs:
- attended: bfloat16 [256, 64, 128], P('pos', 'kvh')
Inputs may be any that keep to these rules, and one draw needn't show every extreme that they name: `suffix_lengths`: each request's suffix, its new token included, holds 1 to 1024 tokens; some request holds exactly 1024.
All inputs are finite; a program needn't handle non-finite values.
Results may differ from a plain program's by a relative error of at most 0.008.
Values may be sent and summed in bfloat16 or wider, within the bound.
A program may use at most 64 MiB of HBM per device.

v0:
```python
import math

import jax
import jax.numpy as jnp
from jax import lax
from jax.sharding import PartitionSpec as P

score_scale = 0.08838834764831845


def on_device(queries, prefix_keys, prefix_values, suffix_keys, suffix_values, suffix_lengths):
    req_count, heads_local, head_size = queries.shape
    groups = prefix_keys.shape[1]
    per_group = heads_local // groups
    suffix_size = suffix_keys.shape[1]
    devices = lax.axis_size("pos")
    gathered = lax.all_gather(queries, "pos", axis=0, tiled=True)
    all_rows = gathered.shape[0]
    row_block = math.gcd(32, all_rows)
    turn_count = all_rows // row_block
    blocked = gathered.reshape(turn_count, row_block, groups, per_group, head_size)

    def prefix_part(query_block):
        scores = (
            jnp.einsum(
                "rgjd,pgd->rgjp", query_block, prefix_keys, preferred_element_type=jnp.float32
            )
            * score_scale
        )
        peak = scores.max(-1)
        weights = jnp.exp(scores - peak[..., None])
        totals = weights.sum(-1)
        summed = jnp.einsum(
            "rgjp,pgd->rgjd",
            weights.astype(jnp.bfloat16),
            prefix_values,
            preferred_element_type=jnp.float32,
        )
        return (peak, totals, summed)

    prefix_peak, prefix_totals, prefix_sums = lax.map(prefix_part, blocked)
    prefix_peak = prefix_peak.reshape(all_rows, heads_local)
    prefix_totals = prefix_totals.reshape(all_rows, heads_local)
    prefix_sums = prefix_sums.reshape(all_rows, heads_local, head_size)
    own_queries = queries.reshape(req_count, groups, per_group, head_size)
    valid = jnp.arange(suffix_size, dtype=jnp.int32)[None, :] < suffix_lengths[:, None]
    valid = valid[:, None, None, :]
    suffix_scores = (
        jnp.einsum("rgjd,rsgd->rgjs", own_queries, suffix_keys, preferred_element_type=jnp.float32)
        * score_scale
    )
    suffix_scores = jnp.where(valid, suffix_scores, -jnp.inf)
    suffix_peak = suffix_scores.max(-1)
    suffix_weights = jnp.where(valid, jnp.exp(suffix_scores - suffix_peak[..., None]), 0.0)
    suffix_totals = suffix_weights.sum(-1).reshape(req_count, heads_local)
    suffix_sums = jnp.einsum(
        "rgjs,rsgd->rgjd",
        suffix_weights.astype(jnp.bfloat16),
        suffix_values,
        preferred_element_type=jnp.float32,
    )
    suffix_sums = suffix_sums.reshape(req_count, heads_local, head_size)
    suffix_peak = suffix_peak.reshape(req_count, heads_local)
    log_total = prefix_peak + jnp.log(prefix_totals)
    normalized = prefix_sums / prefix_totals[..., None]
    got_sums, got_logs = (
        lax.all_to_all(
            normalized.reshape(devices, req_count, heads_local, head_size),
            "pos",
            split_axis=0,
            concat_axis=0,
            tiled=True,
        ),
        lax.all_to_all(
            log_total.reshape(devices, req_count, heads_local),
            "pos",
            split_axis=0,
            concat_axis=0,
            tiled=True,
        ),
    )
    upper = jnp.maximum(got_logs.max(0), suffix_peak)
    source_weight = jnp.exp(got_logs - upper[None])
    suffix_weight = jnp.exp(suffix_peak - upper)
    numerator = (source_weight[..., None] * got_sums).sum(0) + suffix_weight[
        ..., None
    ] * suffix_sums
    denominator = source_weight.sum(0) + suffix_weight * suffix_totals
    return (numerator / denominator[..., None]).astype(jnp.bfloat16)


def solution(mesh):
    return jax.shard_map(
        on_device,
        mesh=mesh,
        in_specs=(
            P("pos", "kvh", None),
            P("pos", "kvh", None),
            P("pos", "kvh", None),
            P("pos", None, "kvh", None),
            P("pos", None, "kvh", None),
            P("pos"),
        ),
        out_specs=P("pos", "kvh", None),
        check_vma=False,
    )
```

profile of v0, /device:TPU:16, one launch (start us, length us, event | category | flops | bytes accessed | tf_op | source)
XLA Modules:
  0.0 228.2 jit_solution(15533742602344683299)
XLA Ops:
  6.5 0.7 all-gather.2.cloned.1.call-update
  7.3 3.4 %copy.22 = bf16[4096,2,128]{2,0,1:T(8,128)(2,1)} copy(bf16[4096,2,128]{2,1,0:T(2,128)(2,1)} %param.9) | data formatting | bytes 4194304 | tf_op jit(solution)/shard_map/while | solution.py:41
  10.7 1.6 copy.23
  12.2 77.1 %all-gather.2.cloned.1.call-done = bf16[256,16,128]{2,1,0:T(8,128)(2,1)} async-done(((bf16[4,16,128]{2,1,0:T(8,128)(2,1)}), bf16[256,16,128]{2,1,0:T(8,128)(2,1)}) %all-gather.2.cloned.1.call-update) | async-done | bytes 1048592 | tf_op jit(solution)/shard_map/all_gather | solution.py:17
  89.3 53.8 %while.14 = (s32[]{:T(128)}, f32[8,32,2,8]{3,2,1,0:T(2,128)S(1)}, f32[8,32,2,8]{3,2,1,0:T(2,128)S(1)}, f32[8,32,2,8,128]{4,3,2,1,0:T(8,128)}, bf16[8,32,2,8,128]...) while((s32[]{:T(128)}, f32[8,32,2,8]{3,2,1,0:T(2,128)S(1)}, ...), condition=%wide.region_3.4_spmd, body=%wide.region_0.3_spmd.sunk | while | flops 1090518016 | bytes 38806644 | solution.py:41
  89.3 3.0 %bitcast_reduce_fusion.2 = (f32[32,2,8]{2,0,1:T(8,128)S(1)}, f32[2,32,8,4096]{3,2,1,0:T(8,128)S(1)}) fusion(bf16[4096,2,128]{2,0,1:T(8,128)(2,1)} %get-tuple-element.164, bf16[8,32,2,8,128]{4,3,2,1,0:T(8,128)(2,1)} %get-tuple-element.163, s32[]{:T(128)} %get-tuple-element.151), kind=kOutput, calls=%fused_computation.1.clone.1 | convolution fusion | flops 541064704 | bytes 10619392 | tf_op jit(solution)/shard_map/while/body/eval_jaxpr/rgjd,pgd->rgjp/dot_general | solution.py:25
  92.3 1.5 fusion.57
  93.8 0.1 copy_dynamic-update-slice_fusion.5
  93.9 0.0 copy-done.1
  93.9 1.4 fusion.58
  95.3 0.7 copy_dynamic-update-slice_fusion.6
  96.0 3.0 %bitcast_reduce_fusion.2 = (f32[32,2,8]{2,0,1:T(8,128)S(1)}, f32[2,32,8,4096]{3,2,1,0:T(8,128)S(1)}) fusion(bf16[4096,2,128]{2,0,1:T(8,128)(2,1)} %get-tuple-element.164, bf16[8,32,2,8,128]{4,3,2,1,0:T(8,128)(2,1)} %get-tuple-element.163, s32[]{:T(128)} %get-tuple-element.151), kind=kOutput, calls=%fused_computation.1.clone.1 | convolution fusion | flops 541064704 | bytes 10619392 | tf_op jit(solution)/shard_map/while/body/eval_jaxpr/rgjd,pgd->rgjp/dot_general | solution.py:25
  99.0 1.5 fusion.57
  100.5 0.1 copy_dynamic-update-slice_fusion.5
  100.6 1.4 fusion.58
  102.0 0.7 copy_dynamic-update-slice_fusion.6
  102.7 3.0 %bitcast_reduce_fusion.2 = (f32[32,2,8]{2,0,1:T(8,128)S(1)}, f32[2,32,8,4096]{3,2,1,0:T(8,128)S(1)}) fusion(bf16[4096,2,128]{2,0,1:T(8,128)(2,1)} %get-tuple-element.164, bf16[8,32,2,8,128]{4,3,2,1,0:T(8,128)(2,1)} %get-tuple-element.163, s32[]{:T(128)} %get-tuple-element.151), kind=kOutput, calls=%fused_computation.1.clone.1 | convolution fusion | flops 541064704 | bytes 10619392 | tf_op jit(solution)/shard_map/while/body/eval_jaxpr/rgjd,pgd->rgjp/dot_general | solution.py:25
  105.7 1.5 fusion.57
  107.2 0.1 copy_dynamic-update-slice_fusion.5
  107.3 1.4 fusion.58
  108.7 0.7 copy_dynamic-update-slice_fusion.6
  109.4 3.0 %bitcast_reduce_fusion.2 = (f32[32,2,8]{2,0,1:T(8,128)S(1)}, f32[2,32,8,4096]{3,2,1,0:T(8,128)S(1)}) fusion(bf16[4096,2,128]{2,0,1:T(8,128)(2,1)} %get-tuple-element.164, bf16[8,32,2,8,128]{4,3,2,1,0:T(8,128)(2,1)} %get-tuple-element.163, s32[]{:T(128)} %get-tuple-element.151), kind=kOutput, calls=%fused_computation.1.clone.1 | convolution fusion | flops 541064704 | bytes 10619392 | tf_op jit(solution)/shard_map/while/body/eval_jaxpr/rgjd,pgd->rgjp/dot_general | solution.py:25
  112.5 1.5 fusion.57
  114.0 0.1 copy_dynamic-update-slice_fusion.5
  114.0 1.4 fusion.58
  115.4 0.7 copy_dynamic-update-slice_fusion.6
  116.2 3.0 %bitcast_reduce_fusion.2 = (f32[32,2,8]{2,0,1:T(8,128)S(1)}, f32[2,32,8,4096]{3,2,1,0:T(8,128)S(1)}) fusion(bf16[4096,2,128]{2,0,1:T(8,128)(2,1)} %get-tuple-element.164, bf16[8,32,2,8,128]{4,3,2,1,0:T(8,128)(2,1)} %get-tuple-element.163, s32[]{:T(128)} %get-tuple-element.151), kind=kOutput, calls=%fused_computation.1.clone.1 | convolution fusion | flops 541064704 | bytes 10619392 | tf_op jit(solution)/shard_map/while/body/eval_jaxpr/rgjd,pgd->rgjp/dot_general | solution.py:25
  119.2 1.5 fusion.57
  120.7 0.1 copy_dynamic-update-slice_fusion.5
  120.8 1.4 fusion.58
  122.2 0.7 copy_dynamic-update-slice_fusion.6
  122.9 3.0 %bitcast_reduce_fusion.2 = (f32[32,2,8]{2,0,1:T(8,128)S(1)}, f32[2,32,8,4096]{3,2,1,0:T(8,128)S(1)}) fusion(bf16[4096,2,128]{2,0,1:T(8,128)(2,1)} %get-tuple-element.164, bf16[8,32,2,8,128]{4,3,2,1,0:T(8,128)(2,1)} %get-tuple-element.163, s32[]{:T(128)} %get-tuple-element.151), kind=kOutput, calls=%fused_computation.1.clone.1 | convolution fusion | flops 541064704 | bytes 10619392 | tf_op jit(solution)/shard_map/while/body/eval_jaxpr/rgjd,pgd->rgjp/dot_general | solution.py:25
  125.9 1.5 fusion.57
  127.4 0.1 copy_dynamic-update-slice_fusion.5
  127.5 1.4 fusion.58
  128.9 0.7 copy_dynamic-update-slice_fusion.6
  129.7 3.0 %bitcast_reduce_fusion.2 = (f32[32,2,8]{2,0,1:T(8,128)S(1)}, f32[2,32,8,4096]{3,2,1,0:T(8,128)S(1)}) fusion(bf16[4096,2,128]{2,0,1:T(8,128)(2,1)} %get-tuple-element.164, bf16[8,32,2,8,128]{4,3,2,1,0:T(8,128)(2,1)} %get-tuple-element.163, s32[]{:T(128)} %get-tuple-element.151), kind=kOutput, calls=%fused_computation.1.clone.1 | convolution fusion | flops 541064704 | bytes 10619392 | tf_op jit(solution)/shard_map/while/body/eval_jaxpr/rgjd,pgd->rgjp/dot_general | solution.py:25
  132.7 1.5 fusion.57
  134.2 0.1 copy_dynamic-update-slice_fusion.5
  134.2 1.4 fusion.58
  135.6 0.7 copy_dynamic-update-slice_fusion.6
  136.4 3.0 %bitcast_reduce_fusion.2 = (f32[32,2,8]{2,0,1:T(8,128)S(1)}, f32[2,32,8,4096]{3,2,1,0:T(8,128)S(1)}) fusion(bf16[4096,2,128]{2,0,1:T(8,128)(2,1)} %get-tuple-element.164, bf16[8,32,2,8,128]{4,3,2,1,0:T(8,128)(2,1)} %get-tuple-element.163, s32[]{:T(128)} %get-tuple-element.151), kind=kOutput, calls=%fused_computation.1.clone.1 | convolution fusion | flops 541064704 | bytes 10619392 | tf_op jit(solution)/shard_map/while/body/eval_jaxpr/rgjd,pgd->rgjp/dot_general | solution.py:25
  139.4 1.5 fusion.57
  140.9 0.1 copy_dynamic-update-slice_fusion.5
  141.0 1.4 fusion.58
  142.4 0.7 copy_dynamic-update-slice_fusion.6
  143.1 0.2 reshape.88
  143.3 0.2 reshape.87
  143.5 0.7 log_add_fusion
  144.2 6.9 %all-to-all-start = ((f32[64,4,16]{2,1,0:T(4,128)}), f32[64,4,16]{2,1,0:T(4,128)S(1)}, u32[]{:S(2)}, u32[]{:S(2)}) async-start(f32[64,4,16]{2,1,0:T(4,128)} %bitcast.56), calls=%async_computation | async-start | bytes 262144 | tf_op jit(solution)/shard_map/all_to_all | solution.py:74
  151.1 3.0 %broadcast_divide_fusion = f32[64,4,16,128]{3,2,1,0:T(8,128)} fusion(f32[64,4,16,128]{3,2,1,0:T(8,128)} %bitcast.12, f32[64,4,16]{2,1,0:T(4,128)S(1)} %reshape.88), kind=kLoop, calls=%fused_computation.30 | loop fusion | flops 524288 | bytes 4210688 | tf_op jit(solution)/shard_map/div | solution.py:65
  154.1 7.3 %all-to-all-done = f32[64,4,16]{2,1,0:T(4,128)S(1)} async-done(((f32[64,4,16]{2,1,0:T(4,128)}), f32[64,4,16]{2,1,0:T(4,128)S(1)}, u32[]{:S(2)}, u32[]{:S(2)}) %all-to-all-start) | async-done | bytes 16416 | tf_op jit(solution)/shard_map/all_to_all | solution.py:74
  161.4 5.6 %all-to-all-start.1 = ((f32[64,4,16,128]{3,2,1,0:T(8,128)}), f32[64,4,16,128]{3,2,1,0:T(8,128)}, u32[]{:S(2)}, u32[]{:S(2)}) async-start(f32[64,4,16,128]{3,2,1,0:T(8,128)} %broadcast_divide_fusion), calls=%async_computation.1 | async-start | bytes 4194304 | tf_op jit(solution)/shard_map/all_to_all | solution.py:67
  167.0 0.1 iota_compare_fusion
  167.1 0.7 fusion.50
  167.8 0.1 reshape.90
  167.9 0.2 fusion.41
  168.1 0.1 reshape.93
  168.2 0.1 reduce_max.27
  168.3 0.1 fusion.49
  168.4 49.6 %all-to-all-done.1 = f32[64,4,16,128]{3,2,1,0:T(8,128)} async-done(((f32[64,4,16,128]{3,2,1,0:T(8,128)}), f32[64,4,16,128]{3,2,1,0:T(8,128)}, u32[]{:S(2)}, u32[]{:S(2)}) %all-to-all-start.1) | async-done | bytes 2097184 | tf_op jit(solution)/shard_map/all_to_all | solution.py:67
  218.0 2.1 multiply_reduce_fusion
  220.1 0.2 copy-done.5
  220.2 1.1 fusion.38
  (30 shorter events, 0.2 us)
Async XLA Ops:
  6.5 160.5 %copy-start = (bf16[4,1024,2,128]{3,2,1,0:T(2,128)(2,1)S(1)}, bf16[4,1024,2,128]{3,2,1,0:T(2,128)(2,1)}, u32[]{:S(2)}) copy-start(bf16[4,1024,2,128]{3,2,1,0:T(2,128)(2,1)} %param.11) | copy-start | bytes 6291460
  6.5 82.7 %all-gather.2.cloned.1.call-start = ((), (), s32[]{:S(2)}) async-start(), calls=%async_computation.2 | async-start | bytes 1064960 | tf_op jit(solution)/shard_map/all_gather | solution.py:17
  7.3 3.4 %copy-start.2 = (bf16[4096,2,128]{2,1,0:T(2,128)(2,1)S(1)}, bf16[4096,2,128]{2,1,0:T(2,128)(2,1)}, u32[]{:S(2)}) copy-start(bf16[4096,2,128]{2,1,0:T(2,128)(2,1)} %param.10) | copy-start | bytes 6291460
  92.3 1.6 copy-start.1
  99.0 1.6 copy-start.1
  105.7 1.6 copy-start.1
  112.4 1.6 copy-start.1
  119.2 1.6 copy-start.1
  125.9 1.6 copy-start.1
  132.7 1.6 copy-start.1
  139.4 1.6 copy-start.1
  144.2 17.2 %all-to-all-start = ((f32[64,4,16]{2,1,0:T(4,128)}), f32[64,4,16]{2,1,0:T(4,128)S(1)}, u32[]{:S(2)}, u32[]{:S(2)}) async-start(f32[64,4,16]{2,1,0:T(4,128)} %bitcast.56), calls=%async_computation | async-start | bytes 262144 | tf_op jit(solution)/shard_map/all_to_all | solution.py:74
  154.1 12.9 %copy-start.4 = (s32[4]{0:T(128)S(1)}, s32[4]{0:T(128)}, u32[]{:S(2)}) copy-start(s32[4]{0:T(128)} %param.13) | copy-start | bytes 52
  154.1 13.0 %copy-start.3 = (bf16[4,16,128]{2,1,0:T(8,128)(2,1)S(1)}, bf16[4,16,128]{2,1,0:T(8,128)(2,1)}, u32[]{:S(2)}) copy-start(bf16[4,16,128]{2,1,0:T(8,128)(2,1)} %param.8) | copy-start | bytes 49156
  161.4 56.6 %all-to-all-start.1 = ((f32[64,4,16,128]{3,2,1,0:T(8,128)}), f32[64,4,16,128]{3,2,1,0:T(8,128)}, u32[]{:S(2)}, u32[]{:S(2)}) async-start(f32[64,4,16,128]{3,2,1,0:T(8,128)} %broadcast_divide_fusion), calls=%async_computation.1 | async-start | bytes 4194304 | tf_op jit(solution)/shard_map/all_to_all | solution.py:67
  218.0 2.2 copy-start.5
Sparse Core Ops, SparseCore 0:
  10.1 79.0 all-gather.1
where the time goes:
time: 230 us; the launch traced here: 228 us
  waiting for transfers between devices  135 us (59%)
  matrix products  37 us (16%)
  other arithmetic  18.2 us (8%)
  between operations  13.5 us (6%)
  starting transfers between devices  12.5 us (5%)
  local copies, waits for them, and re-layouts  12.2 us (5%)
    all_gather x1, waiting for transfers between devices, on_device(): gathered = lax.all_gather(queries, 'pos', axis=0, tiled=True)  77.1 us
    all_to_all x1, waiting for transfers between devices, on_device(): lax.all_to_all(normalized.reshape(devices, req_count, heads_local, head_s...  49.6 us
    dot_general x8, matrix products, prefix_part(): jnp.einsum('rgjd,pgd->rgjp', query_block, prefix_keys, preferred_element_...  24 us
    reduce_sum x8, other arithmetic, prefix_part(): totals = weights.sum(-1)  12 us
    dot_general x8, matrix products, prefix_part(): jnp.einsum('rgjp,pgd->rgjd', weights.astype(jnp.bfloat16), prefix_values,...  11.1 us
    all_to_all x1, waiting for transfers between devices, on_device(): lax.all_to_all(log_total.reshape(devices, req_count, heads_local), 'pos',...  7.33 us
    all_to_all x1, starting transfers between devices, on_device(): lax.all_to_all(log_total.reshape(devices, req_count, heads_local), 'pos',...  6.89 us
    dynamic_update_slice x16, local copies, waits for them, and re-layouts, on_device(): prefix_peak, prefix_totals, prefix_sums = lax.map(prefix_part, blocked)  6.35 us
  transfers between devices with their start and end apart: 3, of which 3 were waited for; matrix products, arithmetic and copies ran while one was open for 4% of the time, Pallas kernels for 0%

commit v1 on v0

v1 whole, which is shorter than its diff:
```python
import functools

import jax
import jax.numpy as jnp
from jax import lax
from jax.experimental import pallas as pl
from jax.experimental.pallas import tpu as pltpu
from jax.sharding import PartitionSpec as P

f32 = jnp.float32
bf16 = jnp.bfloat16
log2e = 1.4426950408889634
scale = 0.08838834764831845 * log2e

X, Z, CORES = 4, 8, 2
REQ, GROUPS, PER, D = 4, 2, 8, 128
ROWS = REQ * PER
KEYS = 4096
SUF = 1024
CHUNKS = 8
LANES = 2 * 4 * ROWS
HALF = LANES // 2
KB = 256
MSG = GROUPS * ROWS + 16
NT = (((1,), (1,)), ((), ()))


def kernel(
    lens, q_ref, k_hbm, v_hbm, sk_hbm, sv_hbm, out_ref,
    kraw, vraw, skraw, svraw, tmp, kg, vt, qall, s_a, s_b, c_a, c_b, res, sib_in, msg_out, msg_in, suf_o, suf_l,
    load_sem, z_send, z_recv, x_send, x_recv, r_send, r_recv, p_send, p_recv, m_send, m_recv,
):
    me = lax.axis_index("pos")
    my_x, my_z, my_core = me // (Z * CORES), (me // CORES) % Z, me % CORES

    def pos_of(dx, dz, dc):
        return (((my_x + dx) % X) * Z + (my_z + dz) % Z) * CORES + (my_core + dc) % CORES

    sibling = {"pos": pos_of(0, 0, 1)}

    loads = [
        pltpu.make_async_copy(src, dst, load_sem.at[n])
        for n, (src, dst) in enumerate(((k_hbm, kraw), (v_hbm, vraw), (sk_hbm, skraw), (sv_hbm, svraw)))
    ]
    for load in loads:
        load.start()

    barrier = pltpu.get_barrier_semaphore()

    def greet(n, carry):
        pl.semaphore_signal(barrier, inc=1, device_id={"pos": pos_of(n // Z, n % Z, 0)}, device_id_type=pl.DeviceIdType.MESH)
        return carry

    lax.fori_loop(1, X * Z, greet, 0)
    pl.semaphore_signal(barrier, inc=1, device_id=sibling, device_id_type=pl.DeviceIdType.MESH)

    mine = q_ref[...].astype(f32).reshape(REQ, GROUPS, PER, D)
    for g in range(GROUPS):
        qall[g, 0, 0, ROWS : 2 * ROWS] = mine[:, g].reshape(ROWS, D).astype(bf16)

    pl.semaphore_wait(barrier, X * Z)

    def z_copy(dz):
        slot = (Z - dz + 1) % Z
        return pltpu.make_async_remote_copy(
            src_ref=qall.at[:, 0, 0, pl.ds(ROWS, ROWS)],
            dst_ref=qall.at[:, 0, slot // 4, pl.ds(pl.multiple_of((slot % 4) * ROWS, ROWS), ROWS)],
            send_sem=z_send.at[dz],
            recv_sem=z_recv.at[Z - dz],
            device_id={"pos": pos_of(0, dz, 0)},
            device_id_type=pl.DeviceIdType.MESH,
        )

    def x_copy(dx):
        return pltpu.make_async_remote_copy(
            src_ref=qall.at[:, 0, :, pl.ds(0, HALF)],
            dst_ref=qall.at[:, X - dx, :, pl.ds(0, HALF)],
            send_sem=x_send.at[dx],
            recv_sem=x_recv.at[X - dx],
            device_id={"pos": pos_of(dx, 0, 0)},
            device_id_type=pl.DeviceIdType.MESH,
        )

    def relay_copy(dx):
        return pltpu.make_async_remote_copy(
            src_ref=qall.at[:, dx, :, pl.ds(0, HALF)],
            dst_ref=qall.at[:, dx, :, pl.ds(HALF, HALF)],
            send_sem=r_send.at[dx],
            recv_sem=r_recv.at[dx],
            device_id=sibling,
            device_id_type=pl.DeviceIdType.MESH,
        )

    def pair_copy(i, g):
        return pltpu.make_async_remote_copy(
            src_ref=res.at[i, g, 1],
            dst_ref=sib_in.at[i, g],
            send_sem=p_send.at[i, g],
            recv_sem=p_recv.at[i, g],
            device_id=sibling,
            device_id_type=pl.DeviceIdType.MESH,
        )

    def msg_copy(dx, dz):
        slot = (dz + 1) % Z
        there = ((X - dx) % X) * Z + (Z - dz) % Z
        return pltpu.make_async_remote_copy(
            src_ref=msg_out.at[dx * Z + slot],
            dst_ref=msg_in.at[there],
            send_sem=m_send.at[dx * Z + dz],
            recv_sem=m_recv.at[there],
            device_id={"pos": pos_of(dx, dz, 0)},
            device_id_type=pl.DeviceIdType.MESH,
        )

    def loop(low, high, do):
        def step(n, carry):
            do(n)
            return carry

        lax.fori_loop(low, high, step, 0)

    loop(1, Z, lambda dz: z_copy(dz).start())

    step = tmp.shape[0]

    def split_keys(n):
        tmp[...] = kraw[pl.ds(pl.multiple_of(n * step, step), step)].astype(f32)
        for g in range(GROUPS):
            kg[g, pl.ds(pl.multiple_of(n * (step // 2), step // 2), step // 2)] = tmp[pl.ds(g, step // 2, stride=2)].astype(bf16)

    def split_values(n):
        tmp[...] = vraw[pl.ds(pl.multiple_of(n * step, step), step)].astype(f32)
        for g in range(GROUPS):
            vt[g, :, pl.ds(pl.multiple_of(n * (step // 2), step // 2), step // 2)] = tmp[pl.ds(g, step // 2, stride=2)].astype(bf16).T

    loads[0].wait()
    loop(0, GROUPS * KEYS // step, split_keys)
    loads[1].wait()
    loop(0, GROUPS * KEYS // step, split_values)

    loop(1, Z, lambda dz: z_copy(Z - dz).wait_recv())
    relay_copy(0).start()
    for dx in (3, 1, 2):
        x_copy(dx).start()

    loads[2].wait()
    loads[3].wait()
    keys = GROUPS * SUF
    row_group = lax.broadcasted_iota(jnp.int32, (GROUPS * PER, keys), 0) // PER
    column = lax.broadcasted_iota(jnp.int32, (GROUPS * PER, keys), 1)
    same_head = row_group == column % GROUPS
    for r in range(REQ):
        rows = pl.ds(r * keys, keys)
        s = lax.dot_general(q_ref[r], skraw[rows], NT, preferred_element_type=f32) * scale
        live = same_head & (column // GROUPS < lens[r])
        s = jnp.where(live, s, -jnp.inf)
        peak = jnp.max(s, axis=1, keepdims=True)
        p = jnp.where(live, jnp.exp2(s - peak), 0.0)
        total = jnp.sum(p, axis=1, keepdims=True)
        o = jnp.dot(p.astype(bf16), svraw[rows], preferred_element_type=f32) / total
        log_total = jnp.broadcast_to(peak + jnp.log(total) * log2e, (GROUPS * PER, D))
        for g in range(GROUPS):
            suf_o[pl.ds(g * ROWS + r * PER, PER)] = o[g * PER : (g + 1) * PER]
            suf_l[pl.ds(g * ROWS + r * PER, PER)] = log_total[g * PER : (g + 1) * PER]

    def phase(qk, pv):
        if qk is not None:
            qv, gq, s_w, c_w = qk
            top = None
        if pv is not None:
            i, gp, s_r, c_r = pv
            c_old = c_r[0:1]
            acc = total = None
        for j in range(KEYS // KB):
            ks = pl.ds(j * KB, KB)
            if qk is not None:
                s = lax.dot_general(kg[gq, ks], qv, NT, preferred_element_type=f32)
                s_w[ks] = s
                m = jnp.max(s.reshape(KB // 8, 8, LANES), axis=0)
                top = m if top is None else jnp.maximum(top, m)
            if pv is not None:
                p = jnp.exp2(s_r[ks] * scale - c_old)
                t = jnp.sum(p.reshape(KB // 8, 8, LANES), axis=0)
                part = jnp.dot(vt[gp, :, ks], p.astype(bf16), preferred_element_type=f32)
                acc = part if acc is None else acc + part
                total = t if total is None else total + t
        if qk is not None:
            c_w[...] = jnp.broadcast_to(jnp.max(top, axis=0, keepdims=True) * scale, c_w.shape)
        if pv is not None:
            sums = jnp.broadcast_to(jnp.sum(total, axis=0, keepdims=True), (8, LANES))
            peaks = jnp.broadcast_to(c_old, (8, LANES))
            for half in range(2):
                lanes = slice(half * HALF, (half + 1) * HALF)
                res[i, gp, half, 0:D] = acc[:, lanes]
                res[i, gp, half, D : D + 8] = peaks[:, lanes]
                res[i, gp, half, D + 8 : D + 16] = sums[:, lanes]
            pair_copy(i, gp).start()

    def queries(g, i):
        return qall[g, i // 2, 1 - i % 2]

    def merge(i):
        dx, half = i // 2, 1 - i % 2
        pieces = []
        for g in range(GROUPS):
            pair_copy(i, g).wait_recv()
            a, b = res.at[i, g, 0], sib_in.at[i, g]
            ca, cb, la, lb = a[D : D + 1], b[D : D + 1], a[D + 8 : D + 9], b[D + 8 : D + 9]
            upper = jnp.maximum(ca, cb)
            wa, wb = jnp.exp2(ca - upper), jnp.exp2(cb - upper)
            total = wa * la + wb * lb
            o = a[0:D] * (wa / total) + b[0:D] * (wb / total)
            rows = o.T.astype(bf16).reshape(4, ROWS, D)
            for n in range(4):
                msg_out[dx * Z + half * 4 + n, g * ROWS : (g + 1) * ROWS] = rows[n]
            log_total = jnp.broadcast_to(upper + jnp.log(total) * log2e, (8, HALF))
            high = log_total.astype(bf16).astype(f32)
            middle = (log_total - high).astype(bf16).astype(f32)
            low = log_total - high - middle
            row = lax.broadcasted_iota(jnp.int32, (8, HALF), 0)
            pieces.append(jnp.where(row == 0, high, jnp.where(row == 1, middle, jnp.where(row == 2, low, 0.0))))
        for n in range(4):
            turned = [p if n == 0 else pltpu.roll(p, HALF - n * ROWS, 1) for p in pieces]
            msg_out[dx * Z + half * 4 + n, GROUPS * ROWS : MSG] = jnp.concatenate(turned, axis=0).astype(bf16)
        for n in range(4):
            if n == 1:

                @pl.when(i == 1)
                def _():
                    msg_in[0] = msg_out[1]

                @pl.when(i != 1)
                def _():
                    msg_copy(dx, (half * 4 + n + Z - 1) % Z).start()
            else:
                msg_copy(dx, (half * 4 + n + Z - 1) % Z).start()

    relay_copy(0).wait_recv()
    phase((queries(0, 0), 0, s_a, c_a), None)

    def chunk(i):
        @pl.when((i % 2 == 1) & (i < CHUNKS - 1))
        def _():
            x_copy(X - (i + 1) // 2).wait_recv()
            relay_copy((i + 1) // 2).start()

        phase((queries(1, i), 1, s_b, c_b), (i, 0, s_a, c_a))

        @pl.when(i > 0)
        def _():
            merge(i - 1)

        @pl.when((i % 2 == 1) & (i < CHUNKS - 1))
        def _():
            relay_copy((i + 1) // 2).wait_recv()

    def full_chunk(i):
        chunk(i)
        phase((queries(0, i + 1), 0, s_a, c_a), (i, 1, s_b, c_b))

    loop(0, CHUNKS - 1, full_chunk)
    last = CHUNKS - 1
    phase((queries(1, last), 1, s_b, c_b), (last, 0, s_a, c_a))
    phase(None, (last, 1, s_b, c_b))
    merge(last - 1)
    merge(last)

    loop(1, Z, lambda dz: z_copy(dz).wait_send())
    loop(1, X, lambda dx: x_copy(dx).wait_send())
    loop(0, X, lambda dx: relay_copy(dx).wait_send())
    for g in range(GROUPS):
        loop(0, CHUNKS, lambda i: pair_copy(i, g).wait_send())
    loop(1, X * Z, lambda n: msg_copy(n // Z, n % Z).wait_send())
    loop(1, X * Z, lambda n: msg_copy(n // Z, n % Z).wait_recv())

    logs = []
    stats = msg_in[:, GROUPS * ROWS : MSG].astype(f32)
    for g in range(GROUPS):
        logs.append(jnp.sum(stats[:, g * 8 : (g + 1) * 8], axis=1).T[0:ROWS])
    logs = jnp.concatenate(logs, axis=0)
    own_log = suf_l[:, 0:1]
    upper = jnp.maximum(jnp.max(logs, axis=1, keepdims=True), own_log)
    weights, own_weight = jnp.exp2(logs - upper), jnp.exp2(own_log - upper)
    total = jnp.sum(weights, axis=1, keepdims=True) + own_weight
    acc = suf_o[...] * own_weight
    for n in range(X * Z):
        acc = acc + weights[:, n : n + 1] * msg_in[n, 0 : GROUPS * ROWS].astype(f32)
    acc = (acc / total).reshape(GROUPS, REQ, PER, D)
    for g in range(GROUPS):
        tmp[pl.ds(g * ROWS, ROWS)] = acc[g].reshape(ROWS, D)
    for r in range(REQ):
        parts = [tmp[pl.ds(g * ROWS + r * PER, PER)] for g in range(GROUPS)]
        out_ref[r] = jnp.concatenate(parts, axis=0).astype(bf16)


def on_device(queries, prefix_keys, prefix_values, suffix_keys, suffix_values, suffix_lengths):
    anywhere = pl.BlockSpec(memory_space=pl.ANY)
    vmem = pl.BlockSpec(memory_space=pltpu.VMEM)
    dma = pltpu.SemaphoreType.DMA
    return pl.pallas_call(
        kernel,
        out_shape=jax.ShapeDtypeStruct(queries.shape, bf16),
        in_specs=[pl.BlockSpec(memory_space=pltpu.SMEM), vmem, anywhere, anywhere, anywhere, anywhere],
        out_specs=vmem,
        scratch_shapes=[
            pltpu.VMEM((GROUPS * KEYS, D), bf16),
            pltpu.VMEM((GROUPS * KEYS, D), bf16),
            pltpu.VMEM((REQ * SUF * GROUPS, D), bf16),
            pltpu.VMEM((REQ * SUF * GROUPS, D), bf16),
            pltpu.VMEM((1024, D), f32),
            pltpu.VMEM((GROUPS, KEYS, D), bf16),
            pltpu.VMEM((GROUPS, D, KEYS), bf16),
            pltpu.VMEM((GROUPS, X, 2, LANES, D), bf16),
            pltpu.VMEM((KEYS, LANES), f32),
            pltpu.VMEM((KEYS, LANES), f32),
            pltpu.VMEM((8, LANES), f32),
            pltpu.VMEM((8, LANES), f32),
            pltpu.VMEM((CHUNKS, GROUPS, 2, D + 16, HALF), f32),
            pltpu.VMEM((CHUNKS, GROUPS, D + 16, HALF), f32),
            pltpu.VMEM((X * Z, MSG, D), bf16),
            pltpu.VMEM((X * Z, MSG, D), bf16),
            pltpu.VMEM((GROUPS * ROWS, D), f32),
            pltpu.VMEM((GROUPS * ROWS, D), f32),
            dma((4,)),
            dma((Z,)), dma((Z,)),
            dma((X,)), dma((X,)),
            dma((X,)), dma((X,)),
            dma((CHUNKS, GROUPS)), dma((CHUNKS, GROUPS)),
            dma((X * Z,)), dma((X * Z,)),
        ],
        compiler_params=pltpu.CompilerParams(collective_id=0, has_side_effects=True, vmem_limit_bytes=56 * 2**20),
        cost_estimate=pl.CostEstimate(flops=9 * 10**9, bytes_accessed=9 * 2**20, transcendentals=17 * 10**6),
    )(
        suffix_lengths,
        queries,
        prefix_keys.reshape(GROUPS * KEYS, D),
        prefix_values.reshape(GROUPS * KEYS, D),
        suffix_keys.reshape(REQ * SUF * GROUPS, D),
        suffix_values.reshape(REQ * SUF * GROUPS, D),
    )


def solution(mesh):
    return jax.shard_map(
        on_device,
        mesh=mesh,
        in_specs=(
            P("pos", "kvh", None),
            P("pos", "kvh", None),
            P("pos", "kvh", None),
            P("pos", None, "kvh", None),
            P("pos", None, "kvh", None),
            P("pos"),
        ),
        out_specs=P("pos", "kvh", None),
        check_vma=False,
    )
```

time: 230 us -> 49.3 us (0.21)
  waiting for transfers between devices: 135 us -> 0 us
  Pallas kernels: 0 us -> 47.4 us
  matrix products: 37 us -> 0 us
  other arithmetic: 18.2 us -> 0 us
  between operations: 13.5 us -> 0.01 us
  starting transfers between devices: 12.5 us -> 0 us
  local copies, waits for them, and re-layouts: 12.2 us -> 1.32 us
    all_gather x1 -> x0, waiting for transfers between devices: 77.1 us -> none  [on_device(): gathered = lax.all_gather(queries, 'pos', axis=0, tiled=True)]
    all_to_all x2 -> x0, waiting for transfers between devices: 57 us -> none  [the longest x1 49.6 us: on_device(): lax.all_to_all(normalized.reshape(devices, req_count, heads_local, head_s...]
    pallas_call x0 -> x1, Pallas kernels: none -> 47.4 us  [on_device(): pl.pallas_call(kernel, out_shape=jax.ShapeDtypeStruct(queries.shape, bf16...]
    dot_general x18 -> x0, matrix products: 37 us -> none  [the longest x8 24 us: prefix_part(): jnp.einsum('rgjd,pgd->rgjp', query_block, prefix_keys, preferred_element_...]
    reduce_sum x11 -> x0, other arithmetic: 14.4 us -> none  [the longest x8 12 us: prefix_part(): totals = weights.sum(-1)]
    all_to_all x2 -> x0, starting transfers between devices: 12.5 us -> none  [the longest x1 6.89 us: on_device(): lax.all_to_all(log_total.reshape(devices, req_count, heads_local), 'pos',...]
    dynamic_update_slice x16 -> x0, local copies, waits for them, and re-layouts: 6.35 us -> none  [on_device(): prefix_peak, prefix_totals, prefix_sums = lax.map(prefix_part, blocked)]
    while x18 -> x0, local copies, waits for them, and re-layouts: 5.08 us -> none  [the longest x2 4.93 us: on_device(): prefix_peak, prefix_totals, prefix_sums = lax.map(prefix_part, blocked)]
  transfers between devices with their start and end apart: 3 -> 0, of which waited for: 3 -> 0; matrix products, arithmetic and copies ran while one was open for 4% -> 0% of each run, Pallas kernels for 0% -> 0%
where the time goes in v1:
time: 49.3 us; the launch traced here: 48.7 us
  Pallas kernels  47.4 us (96%)
  local copies, waits for them, and re-layouts  1.32 us (3%)
    pallas_call x1, Pallas kernels, on_device(): pl.pallas_call(kernel, out_shape=jax.ShapeDtypeStruct(queries.shape, bf16...  47.4 us
    unnamed x1, local copies, waits for them, and re-layouts  1.32 us

profile of v1, /device:TPU:16, one launch (start us, length us, event | category | flops | bytes accessed | tf_op | source)
XLA Modules:
  0.0 48.7 jit_solution(13328004361760102843)
XLA Ops:
  0.0 47.4 %shard_map.64 = bf16[4,16,128]{2,1,0:T(8,128)(2,1)} custom-call(s32[4]{0:T(128)} %lens.1, bf16[4,16,128]{2,1,0:T(8,128)(2,1)} %q_ref.1, bf16[8192,128]{1,0:T(8,128)(2,1)} %bitcast.4, bf16[8192,128]{1,0:T(8,128)(2,1)} %bitcast.5, bf16[8192,128]{1,0:T(8,128)(2,1)} %bitcast.6, bf16[8192,128]{1,0:T(8,128)(2,1)} %bitcast.7), custom_call_target="tpu_custom_call" | custom-call | flops 8999999488 | bytes 9437184 | tf_op jit(solution)/shard_map/pallas_call | solution.py:301
  47.4 1.3 %copy.8 = bf16[4,16,128]{2,1,0:T(8,128)(2,1)} copy(bf16[4,16,128]{2,1,0:T(8,128)(2,1)} %shard_map.64) | data formatting | bytes 32768

commit v2 on v1

--- a/solution.py
+++ b/solution.py
@@ -18,17 +18,20 @@
 KEYS = 4096
 SUF = 1024
 CHUNKS = 8
+ORDER = ((0, 1), (1, 1), (3, 1), (2, 1), (2, 0), (1, 0), (3, 0), (0, 0))
+FAR, NEAR = 1, 0
 LANES = 2 * 4 * ROWS
 HALF = LANES // 2
 KB = 256
 MSG = GROUPS * ROWS + 16
+PART = D + 16
 NT = (((1,), (1,)), ((), ()))
 
 
 def kernel(
     lens, q_ref, k_hbm, v_hbm, sk_hbm, sv_hbm, out_ref,
-    kraw, vraw, skraw, svraw, tmp, kg, vt, qall, s_a, s_b, c_a, c_b, res, sib_in, msg_out, msg_in, suf_o, suf_l,
-    load_sem, z_send, z_recv, x_send, x_recv, r_send, r_recv, p_send, p_recv, m_send, m_recv,
+    kraw, vraw, skraw, svraw, tmp, kg, vt, qall, s_a, s_b, c_a, c_b, res, sib_in, own, x_out, x_in, msg_out, msg_in, suf_o, suf_l,
+    load_sem, z_send, z_recv, x_send, x_recv, r_send, r_recv, p_send, p_recv, xm_send, xm_recv, m_send, m_recv,
 ):
     me = lax.axis_index("pos")
     my_x, my_z, my_core = me // (Z * CORES), (me // CORES) % Z, me % CORES
@@ -47,18 +50,25 @@
 
     barrier = pltpu.get_barrier_semaphore()
 
-    def greet(n, carry):
-        pl.semaphore_signal(barrier, inc=1, device_id={"pos": pos_of(n // Z, n % Z, 0)}, device_id_type=pl.DeviceIdType.MESH)
-        return carry
-
-    lax.fori_loop(1, X * Z, greet, 0)
-    pl.semaphore_signal(barrier, inc=1, device_id=sibling, device_id_type=pl.DeviceIdType.MESH)
+    def loop(low, high, do):
+        def step(n, carry):
+            do(n)
+            return carry
+
+        lax.fori_loop(low, high, step, 0)
+
+    def greet(device):
+        pl.semaphore_signal(barrier, inc=1, device_id=device, device_id_type=pl.DeviceIdType.MESH)
+
+    loop(1, Z, lambda dz: greet({"pos": pos_of(0, dz, 0)}))
+    loop(1, X, lambda dx: greet({"pos": pos_of(dx, 0, 0)}))
+    greet(sibling)
 
     mine = q_ref[...].astype(f32).reshape(REQ, GROUPS, PER, D)
     for g in range(GROUPS):
         qall[g, 0, 0, ROWS : 2 * ROWS] = mine[:, g].reshape(ROWS, D).astype(bf16)
 
-    pl.semaphore_wait(barrier, X * Z)
+    pl.semaphore_wait(barrier, X + Z - 1)
 
     def z_copy(dz):
         slot = (Z - dz + 1) % Z
@@ -71,22 +81,22 @@
             device_id_type=pl.DeviceIdType.MESH,
         )
 
-    def x_copy(dx):
-        return pltpu.make_async_remote_copy(
-            src_ref=qall.at[:, 0, :, pl.ds(0, HALF)],
-            dst_ref=qall.at[:, X - dx, :, pl.ds(0, HALF)],
-            send_sem=x_send.at[dx],
-            recv_sem=x_recv.at[X - dx],
+    def x_copy(dx, half):
+        return pltpu.make_async_remote_copy(
+            src_ref=qall.at[:, 0, half, pl.ds(0, HALF)],
+            dst_ref=qall.at[:, X - dx, half, pl.ds(0, HALF)],
+            send_sem=x_send.at[dx, half],
+            recv_sem=x_recv.at[X - dx, half],
             device_id={"pos": pos_of(dx, 0, 0)},
             device_id_type=pl.DeviceIdType.MESH,
         )
 
-    def relay_copy(dx):
-        return pltpu.make_async_remote_copy(
-            src_ref=qall.at[:, dx, :, pl.ds(0, HALF)],
-            dst_ref=qall.at[:, dx, :, pl.ds(HALF, HALF)],
-            send_sem=r_send.at[dx],
-            recv_sem=r_recv.at[dx],
+    def relay_copy(dx, half):
+        return pltpu.make_async_remote_copy(
+            src_ref=qall.at[:, dx, half, pl.ds(0, HALF)],
+            dst_ref=qall.at[:, dx, half, pl.ds(HALF, HALF)],
+            send_sem=r_send.at[dx, half],
+            recv_sem=r_recv.at[dx, half],
             device_id=sibling,
             device_id_type=pl.DeviceIdType.MESH,
         )
@@ -101,24 +111,25 @@
             device_id_type=pl.DeviceIdType.MESH,
         )
 
-    def msg_copy(dx, dz):
-        slot = (dz + 1) % Z
-        there = ((X - dx) % X) * Z + (Z - dz) % Z
-        return pltpu.make_async_remote_copy(
-            src_ref=msg_out.at[dx * Z + slot],
-            dst_ref=msg_in.at[there],
-            send_sem=m_send.at[dx * Z + dz],
-            recv_sem=m_recv.at[there],
-            device_id={"pos": pos_of(dx, dz, 0)},
-            device_id_type=pl.DeviceIdType.MESH,
-        )
-
-    def loop(low, high, do):
-        def step(n, carry):
-            do(n)
-            return carry
-
-        lax.fori_loop(low, high, step, 0)
+    def part_copy(dx, half, g):
+        return pltpu.make_async_remote_copy(
+            src_ref=x_out.at[dx, half, g],
+            dst_ref=x_in.at[X - dx, half, g],
+            send_sem=xm_send.at[dx, half, g],
+            recv_sem=xm_recv.at[X - dx, half, g],
+            device_id={"pos": pos_of(dx, 0, 0)},
+            device_id_type=pl.DeviceIdType.MESH,
+        )
+
+    def msg_copy(dz):
+        return pltpu.make_async_remote_copy(
+            src_ref=msg_out.at[dz],
+            dst_ref=msg_in.at[Z - dz],
+            send_sem=m_send.at[dz],
+            recv_sem=m_recv.at[Z - dz],
+            device_id={"pos": pos_of(0, dz, 0)},
+            device_id_type=pl.DeviceIdType.MESH,
+        )
 
     loop(1, Z, lambda dz: z_copy(dz).start())
 
@@ -136,24 +147,23 @@
 
     loads[0].wait()
     loop(0, GROUPS * KEYS // step, split_keys)
+
+    loop(1, Z, lambda dz: z_copy(Z - dz).wait_recv())
+    relay_copy(0, FAR).start()
+    for dx, half in ((3, FAR), (1, FAR), (2, FAR), (2, NEAR), (3, NEAR), (1, NEAR)):
+        x_copy(dx, half).start()
+    relay_copy(0, NEAR).start()
+
     loads[1].wait()
     loop(0, GROUPS * KEYS // step, split_values)
 
-    loop(1, Z, lambda dz: z_copy(Z - dz).wait_recv())
-    relay_copy(0).start()
-    for dx in (3, 1, 2):
-        x_copy(dx).start()
-
-    loads[2].wait()
-    loads[3].wait()
-    keys = GROUPS * SUF
-    row_group = lax.broadcasted_iota(jnp.int32, (GROUPS * PER, keys), 0) // PER
-    column = lax.broadcasted_iota(jnp.int32, (GROUPS * PER, keys), 1)
-    same_head = row_group == column % GROUPS
-    for r in range(REQ):
+    def suffix(r):
+        keys = GROUPS * SUF
+        row_group = lax.broadcasted_iota(jnp.int32, (GROUPS * PER, keys), 0) // PER
+        column = lax.broadcasted_iota(jnp.int32, (GROUPS * PER, keys), 1)
+        live = (row_group == column % GROUPS) & (column // GROUPS < lens[r])
         rows = pl.ds(r * keys, keys)
         s = lax.dot_general(q_ref[r], skraw[rows], NT, preferred_element_type=f32) * scale
-        live = same_head & (column // GROUPS < lens[r])
         s = jnp.where(live, s, -jnp.inf)
         peak = jnp.max(s, axis=1, keepdims=True)
         p = jnp.where(live, jnp.exp2(s - peak), 0.0)
@@ -197,82 +207,131 @@
                 res[i, gp, half, D + 8 : D + 16] = sums[:, lanes]
             pair_copy(i, gp).start()
 
+    def place(i):
+        if isinstance(i, int):
+            return ORDER[i]
+        dx, half = 0, 0
+        for n, (a, b) in enumerate(ORDER):
+            dx = jnp.where(i == n, a, dx)
+            half = jnp.where(i == n, b, half)
+        return dx, half
+
     def queries(g, i):
-        return qall[g, i // 2, 1 - i % 2]
-
-    def merge(i):
-        dx, half = i // 2, 1 - i % 2
+        dx, half = place(i)
+        return qall[g, dx, half]
+
+    def in_three(x):
+        high = x.astype(bf16).astype(f32)
+        middle = (x - high).astype(bf16).astype(f32)
+        row = lax.broadcasted_iota(jnp.int32, x.shape, 0)
+        return jnp.where(row == 0, high, jnp.where(row == 1, middle, jnp.where(row == 2, x - high - middle, 0.0)))
+
+    def merge(i, g):
+        dx, half = place(i)
+        pair_copy(i, g).wait_recv()
+        a, b = res.at[i, g, 0], sib_in.at[i, g]
+        ca, cb, la, lb = a[D : D + 1], b[D : D + 1], a[D + 8 : D + 9], b[D + 8 : D + 9]
+        upper = jnp.maximum(ca, cb)
+        wa, wb = jnp.exp2(ca - upper), jnp.exp2(cb - upper)
+        total = wa * la + wb * lb
+        o = a[0:D] * (wa / total) + b[0:D] * (wb / total)
+        log_total = jnp.broadcast_to(upper + jnp.log(total) * log2e, (8, HALF))
+
+        def keep():
+            own[half, g, 0:D] = o
+            own[half, g, D : D + 8] = log_total
+
+        def send():
+            x_out[dx, half, g, 0:D] = o.astype(bf16)
+            x_out[dx, half, g, D:PART] = jnp.concatenate([in_three(log_total), jnp.zeros((8, HALF), f32)], axis=0).astype(bf16)
+            part_copy(dx, half, g).start()
+
+        if isinstance(i, int):
+            keep() if dx == 0 else send()
+        else:
+            pl.when(i == 0)(keep)
+            pl.when(i != 0)(send)
+
+    def merge_x(half):
         pieces = []
         for g in range(GROUPS):
-            pair_copy(i, g).wait_recv()
-            a, b = res.at[i, g, 0], sib_in.at[i, g]
-            ca, cb, la, lb = a[D : D + 1], b[D : D + 1], a[D + 8 : D + 9], b[D + 8 : D + 9]
-            upper = jnp.maximum(ca, cb)
-            wa, wb = jnp.exp2(ca - upper), jnp.exp2(cb - upper)
-            total = wa * la + wb * lb
-            o = a[0:D] * (wa / total) + b[0:D] * (wb / total)
-            rows = o.T.astype(bf16).reshape(4, ROWS, D)
+            for dx in range(1, X):
+                part_copy(X - dx, half, g).wait_recv()
+            logs = [own[half, g, D : D + 1]]
+            logs += [jnp.sum(x_in[dx, half, g, D:PART].astype(f32), axis=0, keepdims=True) for dx in range(1, X)]
+            upper = functools.reduce(jnp.maximum, logs)
+            weights = [jnp.exp2(n - upper) for n in logs]
+            total = sum(weights)
+            o = own[half, g, 0:D] * (weights[0] / total)
+            for dx in range(1, X):
+                o = o + x_in[dx, half, g, 0:D].astype(f32) * (weights[dx] / total)
+            rows = o.T.astype(bf16)
             for n in range(4):
-                msg_out[dx * Z + half * 4 + n, g * ROWS : (g + 1) * ROWS] = rows[n]
-            log_total = jnp.broadcast_to(upper + jnp.log(total) * log2e, (8, HALF))
-            high = log_total.astype(bf16).astype(f32)
-            middle = (log_total - high).astype(bf16).astype(f32)
-            low = log_total - high - middle
-            row = lax.broadcasted_iota(jnp.int32, (8, HALF), 0)
-            pieces.append(jnp.where(row == 0, high, jnp.where(row == 1, middle, jnp.where(row == 2, low, 0.0))))
+                msg_out[(half * 4 + n + Z - 1) % Z, g * ROWS : (g + 1) * ROWS] = rows[n * ROWS : (n + 1) * ROWS]
+            pieces.append(in_three(jnp.broadcast_to(upper + jnp.log(total) * log2e, (8, HALF))))
         for n in range(4):
             turned = [p if n == 0 else pltpu.roll(p, HALF - n * ROWS, 1) for p in pieces]
-            msg_out[dx * Z + half * 4 + n, GROUPS * ROWS : MSG] = jnp.concatenate(turned, axis=0).astype(bf16)
-        for n in range(4):
-            if n == 1:
-
-                @pl.when(i == 1)
-                def _():
-                    msg_in[0] = msg_out[1]
-
-                @pl.when(i != 1)
-                def _():
-                    msg_copy(dx, (half * 4 + n + Z - 1) % Z).start()
+            dz = (half * 4 + n + Z - 1) % Z
+            msg_out[dz, GROUPS * ROWS : MSG] = jnp.concatenate(turned, axis=0).astype(bf16)
+            if dz == 0:
+                msg_in[0] = msg_out[0]
             else:
-                msg_copy(dx, (half * 4 + n + Z - 1) % Z).start()
-
-    relay_copy(0).wait_recv()
+                msg_copy(dz).start()
+
+    relay_copy(0, FAR).wait_recv()
     phase((queries(0, 0), 0, s_a, c_a), None)
 
-    def chunk(i):
-        @pl.when((i % 2 == 1) & (i < CHUNKS - 1))
+    def full_chunk(i):
+        dx, half = place(i + 1)
+
+        @pl.when(i < CHUNKS - 2)
         def _():
-            x_copy(X - (i + 1) // 2).wait_recv()
-            relay_copy((i + 1) // 2).start()
+            x_copy(X - dx, half).wait_recv()
+            relay_copy(dx, half).start()
 
         phase((queries(1, i), 1, s_b, c_b), (i, 0, s_a, c_a))
 
         @pl.when(i > 0)
         def _():
-            merge(i - 1)
-
-        @pl.when((i % 2 == 1) & (i < CHUNKS - 1))
+            merge(i - 1, 0)
+
+        @pl.when(i == CHUNKS - 2)
         def _():
-            relay_copy((i + 1) // 2).wait_recv()
-
-    def full_chunk(i):
-        chunk(i)
+            merge_x(FAR)
+
+        relay_copy(dx, half).wait_recv()
         phase((queries(0, i + 1), 0, s_a, c_a), (i, 1, s_b, c_b))
+
+        @pl.when(i > 0)
+        def _():
+            merge(i - 1, 1)
 
     loop(0, CHUNKS - 1, full_chunk)
     last = CHUNKS - 1
     phase((queries(1, last), 1, s_b, c_b), (last, 0, s_a, c_a))
+    merge(last - 1, 0)
+    merge(last - 1, 1)
     phase(None, (last, 1, s_b, c_b))
-    merge(last - 1)
-    merge(last)
+    loads[2].wait()
+    loads[3].wait()
+    suffix(0)
+    merge(last, 0)
+    suffix(1)
+    merge(last, 1)
+    merge_x(NEAR)
+    suffix(2)
+    suffix(3)
 
     loop(1, Z, lambda dz: z_copy(dz).wait_send())
-    loop(1, X, lambda dx: x_copy(dx).wait_send())
-    loop(0, X, lambda dx: relay_copy(dx).wait_send())
+    for half in range(2):
+        loop(1, X, lambda dx: x_copy(dx, half).wait_send())
+        loop(0, X, lambda dx: relay_copy(dx, half).wait_send())
+        for g in range(GROUPS):
+            loop(1, X, lambda dx: part_copy(dx, half, g).wait_send())
     for g in range(GROUPS):
         loop(0, CHUNKS, lambda i: pair_copy(i, g).wait_send())
-    loop(1, X * Z, lambda n: msg_copy(n // Z, n % Z).wait_send())
-    loop(1, X * Z, lambda n: msg_copy(n // Z, n % Z).wait_recv())
+    loop(1, Z, lambda dz: msg_copy(dz).wait_send())
+    loop(1, Z, lambda dz: msg_copy(dz).wait_recv())
 
     logs = []
     stats = msg_in[:, GROUPS * ROWS : MSG].astype(f32)
@@ -284,7 +343,7 @@
     weights, own_weight = jnp.exp2(logs - upper), jnp.exp2(own_log - upper)
     total = jnp.sum(weights, axis=1, keepdims=True) + own_weight
     acc = suf_o[...] * own_weight
-    for n in range(X * Z):
+    for n in range(Z):
         acc = acc + weights[:, n : n + 1] * msg_in[n, 0 : GROUPS * ROWS].astype(f32)
     acc = (acc / total).reshape(GROUPS, REQ, PER, D)
     for g in range(GROUPS):
@@ -318,16 +377,20 @@
             pltpu.VMEM((8, LANES), f32),
             pltpu.VMEM((CHUNKS, GROUPS, 2, D + 16, HALF), f32),
             pltpu.VMEM((CHUNKS, GROUPS, D + 16, HALF), f32),
-            pltpu.VMEM((X * Z, MSG, D), bf16),
-            pltpu.VMEM((X * Z, MSG, D), bf16),
+            pltpu.VMEM((2, GROUPS, D + 8, HALF), f32),
+            pltpu.VMEM((X, 2, GROUPS, PART, HALF), bf16),
+            pltpu.VMEM((X, 2, GROUPS, PART, HALF), bf16),
+            pltpu.VMEM((Z, MSG, D), bf16),
+            pltpu.VMEM((Z, MSG, D), bf16),
             pltpu.VMEM((GROUPS * ROWS, D), f32),
             pltpu.VMEM((GROUPS * ROWS, D), f32),
             dma((4,)),
             dma((Z,)), dma((Z,)),
-            dma((X,)), dma((X,)),
-            dma((X,)), dma((X,)),
+            dma((X, 2)), dma((X, 2)),
+            dma((X, 2)), dma((X, 2)),
             dma((CHUNKS, GROUPS)), dma((CHUNKS, GROUPS)),
-            dma((X * Z,)), dma((X * Z,)),
+            dma((X, 2, GROUPS)), dma((X, 2, GROUPS)),
+            dma((Z,)), dma((Z,)),
         ],
         compiler_params=pltpu.CompilerParams(collective_id=0, has_side_effects=True, vmem_limit_bytes=56 * 2**20),
         cost_estimate=pl.CostEstimate(flops=9 * 10**9, bytes_accessed=9 * 2**20, transcendentals=17 * 10**6),

time: 49.3 us -> 47 us (0.953)
  Pallas kernels: 47.4 us -> 45.4 us
    pallas_call x1, Pallas kernels: 47.4 us -> 45.4 us  [on_device(): pl.pallas_call(kernel, out_shape=jax.ShapeDtypeStruct(queries.shape, bf16...]
where the time goes in v2:
time: 47 us; the launch traced here: 46.8 us
  Pallas kernels  45.4 us (97%)
  local copies, waits for them, and re-layouts  1.32 us (3%)
    pallas_call x1, Pallas kernels, on_device(): pl.pallas_call(kernel, out_shape=jax.ShapeDtypeStruct(queries.shape, bf16...  45.4 us
    unnamed x1, local copies, waits for them, and re-layouts  1.32 us

profile of v2, /device:TPU:16, one launch (start us, length us, event | category | flops | bytes accessed | tf_op | source)
XLA Modules:
  0.0 46.8 jit_solution(66534663897273351)
XLA Ops:
  0.0 45.4 %shard_map.64 = bf16[4,16,128]{2,1,0:T(8,128)(2,1)} custom-call(s32[4]{0:T(128)} %lens.1, bf16[4,16,128]{2,1,0:T(8,128)(2,1)} %q_ref.1, bf16[8192,128]{1,0:T(8,128)(2,1)} %bitcast.4, bf16[8192,128]{1,0:T(8,128)(2,1)} %bitcast.5, bf16[8192,128]{1,0:T(8,128)(2,1)} %bitcast.6, bf16[8192,128]{1,0:T(8,128)(2,1)} %bitcast.7), custom_call_target="tpu_custom_call" | custom-call | flops 8999999488 | bytes 9437184 | tf_op jit(solution)/shard_map/pallas_call | solution.py:360
  45.5 1.3 %copy.8 = bf16[4,16,128]{2,1,0:T(8,128)(2,1)} copy(bf16[4,16,128]{2,1,0:T(8,128)(2,1)} %shard_map.64) | data formatting | bytes 32768

commit v3 on v2

--- a/solution.py
+++ b/solution.py
@@ -18,12 +18,12 @@
 KEYS = 4096
 SUF = 1024
 CHUNKS = 8
-ORDER = ((0, 1), (1, 1), (3, 1), (2, 1), (2, 0), (1, 0), (3, 0), (0, 0))
+ORDER = ((0, 0), (1, 0), (3, 0), (2, 0), (1, 1), (2, 1), (3, 1), (0, 1))
 FAR, NEAR = 1, 0
 LANES = 2 * 4 * ROWS
 HALF = LANES // 2
 KB = 256
-MSG = GROUPS * ROWS + 16
+MSG = ROWS + 16
 PART = D + 16
 NT = (((1,), (1,)), ((), ()))
 
@@ -121,17 +121,18 @@
             device_id_type=pl.DeviceIdType.MESH,
         )
 
-    def msg_copy(dz):
-        return pltpu.make_async_remote_copy(
-            src_ref=msg_out.at[dz],
-            dst_ref=msg_in.at[Z - dz],
-            send_sem=m_send.at[dz],
-            recv_sem=m_recv.at[Z - dz],
+    def msg_copy(dz, g):
+        return pltpu.make_async_remote_copy(
+            src_ref=msg_out.at[g, dz],
+            dst_ref=msg_in.at[g, Z - dz],
+            send_sem=m_send.at[g, dz],
+            recv_sem=m_recv.at[g, Z - dz],
             device_id={"pos": pos_of(0, dz, 0)},
             device_id_type=pl.DeviceIdType.MESH,
         )
 
-    loop(1, Z, lambda dz: z_copy(dz).start())
+    for dz in (1, 7, 2, 6, 3, 5, 4):
+        z_copy(dz).start()
 
     step = tmp.shape[0]
 
@@ -148,12 +149,14 @@
     loads[0].wait()
     loop(0, GROUPS * KEYS // step, split_keys)
 
-    loop(1, Z, lambda dz: z_copy(Z - dz).wait_recv())
-    relay_copy(0, FAR).start()
-    for dx, half in ((3, FAR), (1, FAR), (2, FAR), (2, NEAR), (3, NEAR), (1, NEAR)):
-        x_copy(dx, half).start()
-    relay_copy(0, NEAR).start()
-
+    def pass_on(half):
+        for dz in (3, 4, 5, 6) if half == FAR else (7, 1, 2):
+            z_copy(Z - dz).wait_recv()
+        relay_copy(0, half).start()
+        for dx in (3, 1, 2):
+            x_copy(dx, half).start()
+
+    pass_on(NEAR)
     loads[1].wait()
     loop(0, GROUPS * KEYS // step, split_values)
 
@@ -252,59 +255,68 @@
             pl.when(i == 0)(keep)
             pl.when(i != 0)(send)
 
-    def merge_x(half):
-        pieces = []
-        for g in range(GROUPS):
-            for dx in range(1, X):
-                part_copy(X - dx, half, g).wait_recv()
-            logs = [own[half, g, D : D + 1]]
-            logs += [jnp.sum(x_in[dx, half, g, D:PART].astype(f32), axis=0, keepdims=True) for dx in range(1, X)]
-            upper = functools.reduce(jnp.maximum, logs)
-            weights = [jnp.exp2(n - upper) for n in logs]
-            total = sum(weights)
-            o = own[half, g, 0:D] * (weights[0] / total)
-            for dx in range(1, X):
-                o = o + x_in[dx, half, g, 0:D].astype(f32) * (weights[dx] / total)
-            rows = o.T.astype(bf16)
-            for n in range(4):
-                msg_out[(half * 4 + n + Z - 1) % Z, g * ROWS : (g + 1) * ROWS] = rows[n * ROWS : (n + 1) * ROWS]
-            pieces.append(in_three(jnp.broadcast_to(upper + jnp.log(total) * log2e, (8, HALF))))
-        for n in range(4):
-            turned = [p if n == 0 else pltpu.roll(p, HALF - n * ROWS, 1) for p in pieces]
+    def merge_x(half, g):
+        for dx in range(1, X):
+            part_copy(X - dx, half, g).wait_recv()
+        logs = [own[half, g, D : D + 1]]
+        logs += [jnp.sum(x_in[dx, half, g, D:PART].astype(f32), axis=0, keepdims=True) for dx in range(1, X)]
+        upper = functools.reduce(jnp.maximum, logs)
+        weights = [jnp.exp2(n - upper) for n in logs]
+        total = sum(weights)
+        o = own[half, g, 0:D] * (weights[0] / total)
+        for dx in range(1, X):
+            o = o + x_in[dx, half, g, 0:D].astype(f32) * (weights[dx] / total)
+        rows = o.T.astype(bf16)
+        piece = in_three(jnp.broadcast_to(upper + jnp.log(total) * log2e, (8, HALF)))
+        for n in (3, 0, 2, 1):
             dz = (half * 4 + n + Z - 1) % Z
-            msg_out[dz, GROUPS * ROWS : MSG] = jnp.concatenate(turned, axis=0).astype(bf16)
+            turned = piece if n == 0 else pltpu.roll(piece, HALF - n * ROWS, 1)
+            msg_out[g, dz, 0:ROWS] = rows[n * ROWS : (n + 1) * ROWS]
+            msg_out[g, dz, ROWS:MSG] = jnp.concatenate([turned, jnp.zeros((8, HALF), f32)], axis=0).astype(bf16)
             if dz == 0:
-                msg_in[0] = msg_out[0]
+                msg_in[g, 0] = msg_out[g, 0]
             else:
-                msg_copy(dz).start()
-
-    relay_copy(0, FAR).wait_recv()
+                msg_copy(dz, g).start()
+
+    def relay(i):
+        dx, half = place(i)
+        x_copy(X - dx, half).wait_recv()
+        relay_copy(dx, half).start()
+
+    relay_copy(0, NEAR).wait_recv()
     phase((queries(0, 0), 0, s_a, c_a), None)
+    relay(1)
 
     def full_chunk(i):
+        phase((queries(1, i), 1, s_b, c_b), (i, 0, s_a, c_a))
+
+        @pl.when(i == 0)
+        def _():
+            pass_on(FAR)
+
+        @pl.when(i > 0)
+        def _():
+            merge(i - 1, 0)
+
+        @pl.when(i == CHUNKS - 3)
+        def _():
+            merge_x(NEAR, 0)
+
+        @pl.when(i < CHUNKS - 3)
+        def _():
+            relay(i + 2)
+
         dx, half = place(i + 1)
-
-        @pl.when(i < CHUNKS - 2)
-        def _():
-            x_copy(X - dx, half).wait_recv()
-            relay_copy(dx, half).start()
-
-        phase((queries(1, i), 1, s_b, c_b), (i, 0, s_a, c_a))
-
-        @pl.when(i > 0)
-        def _():
-            merge(i - 1, 0)
-
-        @pl.when(i == CHUNKS - 2)
-        def _():
-            merge_x(FAR)
-
         relay_copy(dx, half).wait_recv()
         phase((queries(0, i + 1), 0, s_a, c_a), (i, 1, s_b, c_b))
 
         @pl.when(i > 0)
         def _():
             merge(i - 1, 1)
+
+        @pl.when(i == CHUNKS - 3)
+        def _():
+            merge_x(NEAR, 1)
 
     loop(0, CHUNKS - 1, full_chunk)
     last = CHUNKS - 1
@@ -316,9 +328,10 @@
     loads[3].wait()
     suffix(0)
     merge(last, 0)
+    merge_x(FAR, 0)
     suffix(1)
     merge(last, 1)
-    merge_x(NEAR)
+    merge_x(FAR, 1)
     suffix(2)
     suffix(3)
 
@@ -330,13 +343,13 @@
             loop(1, X, lambda dx: part_copy(dx, half, g).wait_send())
     for g in range(GROUPS):
         loop(0, CHUNKS, lambda i: pair_copy(i, g).wait_send())
-    loop(1, Z, lambda dz: msg_copy(dz).wait_send())
-    loop(1, Z, lambda dz: msg_copy(dz).wait_recv())
+    for g in range(GROUPS):
+        loop(1, Z, lambda dz: msg_copy(dz, g).wait_send())
+        loop(1, Z, lambda dz: msg_copy(dz, g).wait_recv())
 
     logs = []
-    stats = msg_in[:, GROUPS * ROWS : MSG].astype(f32)
     for g in range(GROUPS):
-        logs.append(jnp.sum(stats[:, g * 8 : (g + 1) * 8], axis=1).T[0:ROWS])
+        logs.append(jnp.sum(msg_in[g, :, ROWS:MSG].astype(f32), axis=1).T[0:ROWS])
     logs = jnp.concatenate(logs, axis=0)
     own_log = suf_l[:, 0:1]
     upper = jnp.maximum(jnp.max(logs, axis=1, keepdims=True), own_log)
@@ -344,7 +357,7 @@
     total = jnp.sum(weights, axis=1, keepdims=True) + own_weight
     acc = suf_o[...] * own_weight
     for n in range(Z):
-        acc = acc + weights[:, n : n + 1] * msg_in[n, 0 : GROUPS * ROWS].astype(f32)
+        acc = acc + weights[:, n : n + 1] * msg_in[:, n, 0:ROWS].astype(f32).reshape(GROUPS * ROWS, D)
     acc = (acc / total).reshape(GROUPS, REQ, PER, D)
     for g in range(GROUPS):
         tmp[pl.ds(g * ROWS, ROWS)] = acc[g].reshape(ROWS, D)
@@ -380,8 +393,8 @@
             pltpu.VMEM((2, GROUPS, D + 8, HALF), f32),
             pltpu.VMEM((X, 2, GROUPS, PART, HALF), bf16),
             pltpu.VMEM((X, 2, GROUPS, PART, HALF), bf16),
-            pltpu.VMEM((Z, MSG, D), bf16),
-            pltpu.VMEM((Z, MSG, D), bf16),
+            pltpu.VMEM((GROUPS, Z, MSG, D), bf16),
+            pltpu.VMEM((GROUPS, Z, MSG, D), bf16),
             pltpu.VMEM((GROUPS * ROWS, D), f32),
             pltpu.VMEM((GROUPS * ROWS, D), f32),
             dma((4,)),
@@ -390,7 +403,7 @@
             dma((X, 2)), dma((X, 2)),
             dma((CHUNKS, GROUPS)), dma((CHUNKS, GROUPS)),
             dma((X, 2, GROUPS)), dma((X, 2, GROUPS)),
-            dma((Z,)), dma((Z,)),
+            dma((GROUPS, Z)), dma((GROUPS, Z)),
         ],
         compiler_params=pltpu.CompilerParams(collective_id=0, has_side_effects=True, vmem_limit_bytes=56 * 2**20),
         cost_estimate=pl.CostEstimate(flops=9 * 10**9, bytes_accessed=9 * 2**20, transcendentals=17 * 10**6),

time: 47 us -> 47.6 us (1.013); the launches traced: 46.8 us -> 46.9 us
  no operation moved by 1% of the time
where the time goes in v3:
time: 47.6 us; the launch traced here: 46.9 us
  Pallas kernels  45.5 us (96%)
  local copies, waits for them, and re-layouts  1.32 us (3%)
    pallas_call x1, Pallas kernels, on_device(): pl.pallas_call(kernel, out_shape=jax.ShapeDtypeStruct(queries.shape, bf16...  45.5 us
    unnamed x1, local copies, waits for them, and re-layouts  1.32 us

profile of v3, /device:TPU:16, one launch (start us, length us, event | category | flops | bytes accessed | tf_op | source)
XLA Modules:
  0.0 46.9 jit_solution(6122400735251848361)
XLA Ops:
  0.0 45.5 %shard_map.64 = bf16[4,16,128]{2,1,0:T(8,128)(2,1)} custom-call(s32[4]{0:T(128)} %lens.1, bf16[4,16,128]{2,1,0:T(8,128)(2,1)} %q_ref.1, bf16[8192,128]{1,0:T(8,128)(2,1)} %bitcast.4, bf16[8192,128]{1,0:T(8,128)(2,1)} %bitcast.5, bf16[8192,128]{1,0:T(8,128)(2,1)} %bitcast.6, bf16[8192,128]{1,0:T(8,128)(2,1)} %bitcast.7), custom_call_target="tpu_custom_call" | custom-call | flops 8999999488 | bytes 9437184 | tf_op jit(solution)/shard_map/pallas_call | solution.py:373
  45.5 1.3 %copy.8 = bf16[4,16,128]{2,1,0:T(8,128)(2,1)} copy(bf16[4,16,128]{2,1,0:T(8,128)(2,1)} %shard_map.64) | data formatting | bytes 32768

commit v4 on v3

--- a/solution.py
+++ b/solution.py
@@ -20,6 +20,7 @@
 CHUNKS = 8
 ORDER = ((0, 0), (1, 0), (3, 0), (2, 0), (1, 1), (2, 1), (3, 1), (0, 1))
 FAR, NEAR = 1, 0
+SIDE = (0, 7, 1, 6)
 LANES = 2 * 4 * ROWS
 HALF = LANES // 2
 KB = 256
@@ -31,7 +32,7 @@
 def kernel(
     lens, q_ref, k_hbm, v_hbm, sk_hbm, sv_hbm, out_ref,
     kraw, vraw, skraw, svraw, tmp, kg, vt, qall, s_a, s_b, c_a, c_b, res, sib_in, own, x_out, x_in, msg_out, msg_in, suf_o, suf_l,
-    load_sem, z_send, z_recv, x_send, x_recv, r_send, r_recv, p_send, p_recv, xm_send, xm_recv, m_send, m_recv,
+    load_sem, z_send, z_recv, d_send, d_recv, x_send, x_recv, r_send, r_recv, p_send, p_recv, xm_send, xm_recv, m_send, m_recv,
 ):
     me = lax.axis_index("pos")
     my_x, my_z, my_core = me // (Z * CORES), (me // CORES) % Z, me % CORES
@@ -63,12 +64,14 @@
     loop(1, Z, lambda dz: greet({"pos": pos_of(0, dz, 0)}))
     loop(1, X, lambda dx: greet({"pos": pos_of(dx, 0, 0)}))
     greet(sibling)
+    for dz in SIDE[1:]:
+        greet({"pos": pos_of(1, Z - dz, 0)})
 
     mine = q_ref[...].astype(f32).reshape(REQ, GROUPS, PER, D)
     for g in range(GROUPS):
         qall[g, 0, 0, ROWS : 2 * ROWS] = mine[:, g].reshape(ROWS, D).astype(bf16)
 
-    pl.semaphore_wait(barrier, X + Z - 1)
+    pl.semaphore_wait(barrier, X + Z - 1 + len(SIDE) - 1)
 
     def z_copy(dz):
         slot = (Z - dz + 1) % Z
@@ -81,6 +84,17 @@
             device_id_type=pl.DeviceIdType.MESH,
         )
 
+    def side_copy(dz):
+        slot = (Z - dz + 1) % Z
+        return pltpu.make_async_remote_copy(
+            src_ref=qall.at[:, 0, NEAR, pl.ds(ROWS, ROWS)],
+            dst_ref=qall.at[:, 1, NEAR, pl.ds(slot * ROWS, ROWS)],
+            send_sem=d_send.at[slot],
+            recv_sem=d_recv.at[slot],
+            device_id={"pos": pos_of(X - 1, dz, 0)},
+            device_id_type=pl.DeviceIdType.MESH,
+        )
+
     def x_copy(dx, half):
         return pltpu.make_async_remote_copy(
             src_ref=qall.at[:, 0, half, pl.ds(0, HALF)],
@@ -131,7 +145,11 @@
             device_id_type=pl.DeviceIdType.MESH,
         )
 
-    for dz in (1, 7, 2, 6, 3, 5, 4):
+    for dz in (1, 7, 2):
+        z_copy(dz).start()
+    for dz in SIDE:
+        side_copy(dz).start()
+    for dz in (6, 3, 5, 4):
         z_copy(dz).start()
 
     step = tmp.shape[0]
@@ -148,17 +166,17 @@
 
     loads[0].wait()
     loop(0, GROUPS * KEYS // step, split_keys)
+    loads[1].wait()
+    loop(0, GROUPS * KEYS // step, split_values)
 
     def pass_on(half):
         for dz in (3, 4, 5, 6) if half == FAR else (7, 1, 2):
             z_copy(Z - dz).wait_recv()
         relay_copy(0, half).start()
-        for dx in (3, 1, 2):
+        for dx in (3, 1, 2) if half == FAR else (1, 2):
             x_copy(dx, half).start()
 
     pass_on(NEAR)
-    loads[1].wait()
-    loop(0, GROUPS * KEYS // step, split_values)
 
     def suffix(r):
         keys = GROUPS * SUF
@@ -285,14 +303,12 @@
 
     relay_copy(0, NEAR).wait_recv()
     phase((queries(0, 0), 0, s_a, c_a), None)
-    relay(1)
+    for dz in SIDE:
+        side_copy(dz).wait_recv()
+    relay_copy(1, NEAR).start()
 
     def full_chunk(i):
         phase((queries(1, i), 1, s_b, c_b), (i, 0, s_a, c_a))
-
-        @pl.when(i == 0)
-        def _():
-            pass_on(FAR)
 
         @pl.when(i > 0)
         def _():
@@ -310,6 +326,10 @@
         relay_copy(dx, half).wait_recv()
         phase((queries(0, i + 1), 0, s_a, c_a), (i, 1, s_b, c_b))
 
+        @pl.when(i == 0)
+        def _():
+            pass_on(FAR)
+
         @pl.when(i > 0)
         def _():
             merge(i - 1, 1)
@@ -320,24 +340,26 @@
 
     loop(0, CHUNKS - 1, full_chunk)
     last = CHUNKS - 1
+    merge(last - 1, 0)
     phase((queries(1, last), 1, s_b, c_b), (last, 0, s_a, c_a))
-    merge(last - 1, 0)
     merge(last - 1, 1)
     phase(None, (last, 1, s_b, c_b))
     loads[2].wait()
     loads[3].wait()
     suffix(0)
     merge(last, 0)
-    merge_x(FAR, 0)
     suffix(1)
     merge(last, 1)
+    merge_x(FAR, 0)
+    suffix(2)
     merge_x(FAR, 1)
-    suffix(2)
     suffix(3)
 
+    for dz in SIDE:
+        side_copy(dz).wait_send()
     loop(1, Z, lambda dz: z_copy(dz).wait_send())
     for half in range(2):
-        loop(1, X, lambda dx: x_copy(dx, half).wait_send())
+        loop(1, X if half == FAR else X - 1, lambda dx: x_copy(dx, half).wait_send())
         loop(0, X, lambda dx: relay_copy(dx, half).wait_send())
         for g in range(GROUPS):
             loop(1, X, lambda dx: part_copy(dx, half, g).wait_send())
@@ -399,6 +421,7 @@
             pltpu.VMEM((GROUPS * ROWS, D), f32),
             dma((4,)),
             dma((Z,)), dma((Z,)),
+            dma((4,)), dma((4,)),
             dma((X, 2)), dma((X, 2)),
             dma((X, 2)), dma((X, 2)),
             dma((CHUNKS, GROUPS)), dma((CHUNKS, GROUPS)),

time: 47.6 us -> 48.6 us (1.021)
  Pallas kernels: 45.5 us -> 46.6 us
    pallas_call x1, Pallas kernels: 45.5 us -> 46.6 us  [on_device(): pl.pallas_call(kernel, out_shape=jax.ShapeDtypeStruct(queries.shape, bf16...]
where the time goes in v4:
time: 48.6 us; the launch traced here: 47.9 us
  Pallas kernels  46.6 us (96%)
  local copies, waits for them, and re-layouts  1.32 us (3%)
    pallas_call x1, Pallas kernels, on_device(): pl.pallas_call(kernel, out_shape=jax.ShapeDtypeStruct(queries.shape, bf16...  46.6 us
    unnamed x1, local copies, waits for them, and re-layouts  1.32 us

profile of v4, /device:TPU:16, one launch (start us, length us, event | category | flops | bytes accessed | tf_op | source)
XLA Modules:
  0.0 47.9 jit_solution(12703052501222991232)
XLA Ops:
  0.0 46.6 %shard_map.64 = bf16[4,16,128]{2,1,0:T(8,128)(2,1)} custom-call(s32[4]{0:T(128)} %lens.1, bf16[4,16,128]{2,1,0:T(8,128)(2,1)} %q_ref.1, bf16[8192,128]{1,0:T(8,128)(2,1)} %bitcast.4, bf16[8192,128]{1,0:T(8,128)(2,1)} %bitcast.5, bf16[8192,128]{1,0:T(8,128)(2,1)} %bitcast.6, bf16[8192,128]{1,0:T(8,128)(2,1)} %bitcast.7), custom_call_target="tpu_custom_call" | custom-call | flops 8999999488 | bytes 9437184 | tf_op jit(solution)/shard_map/pallas_call | solution.py:395
  46.6 1.3 %copy.8 = bf16[4,16,128]{2,1,0:T(8,128)(2,1)} copy(bf16[4,16,128]{2,1,0:T(8,128)(2,1)} %shard_map.64) | data formatting | bytes 32768

commit v5 on v2

--- a/solution.py
+++ b/solution.py
@@ -131,7 +131,8 @@
             device_id_type=pl.DeviceIdType.MESH,
         )
 
-    loop(1, Z, lambda dz: z_copy(dz).start())
+    for dz in (4, 3, 5, 6, 2, 1, 7):
+        z_copy(dz).start()
 
     step = tmp.shape[0]
 
@@ -148,10 +149,15 @@
     loads[0].wait()
     loop(0, GROUPS * KEYS // step, split_keys)
 
-    loop(1, Z, lambda dz: z_copy(Z - dz).wait_recv())
+    for dz in (3, 4, 5, 6):
+        z_copy(Z - dz).wait_recv()
     relay_copy(0, FAR).start()
-    for dx, half in ((3, FAR), (1, FAR), (2, FAR), (2, NEAR), (3, NEAR), (1, NEAR)):
-        x_copy(dx, half).start()
+    for dx in (3, 1, 2):
+        x_copy(dx, FAR).start()
+    for dz in (7, 1, 2):
+        z_copy(Z - dz).wait_recv()
+    for dx in (2, 3, 1):
+        x_copy(dx, NEAR).start()
     relay_copy(0, NEAR).start()
 
     loads[1].wait()
@@ -312,13 +318,13 @@
     merge(last - 1, 0)
     merge(last - 1, 1)
     phase(None, (last, 1, s_b, c_b))
+    merge(last, 0)
+    merge(last, 1)
+    merge_x(NEAR)
     loads[2].wait()
     loads[3].wait()
     suffix(0)
-    merge(last, 0)
     suffix(1)
-    merge(last, 1)
-    merge_x(NEAR)
     suffix(2)
     suffix(3)
 

time: 47 us -> 46.4 us (0.987)
  Pallas kernels: 45.4 us -> 44.8 us
    pallas_call x1, Pallas kernels: 45.4 us -> 44.8 us  [on_device(): pl.pallas_call(kernel, out_shape=jax.ShapeDtypeStruct(queries.shape, bf16...]
where the time goes in v5:
time: 46.4 us; the launch traced here: 46.1 us
  Pallas kernels  44.8 us (97%)
  local copies, waits for them, and re-layouts  1.32 us (3%)
    pallas_call x1, Pallas kernels, on_device(): pl.pallas_call(kernel, out_shape=jax.ShapeDtypeStruct(queries.shape, bf16...  44.8 us
    unnamed x1, local copies, waits for them, and re-layouts  1.32 us

profile of v5, /device:TPU:16, one launch (start us, length us, event | category | flops | bytes accessed | tf_op | source)
XLA Modules:
  0.0 46.1 jit_solution(9987391585419071781)
XLA Ops:
  0.0 44.8 %shard_map.64 = bf16[4,16,128]{2,1,0:T(8,128)(2,1)} custom-call(s32[4]{0:T(128)} %lens.1, bf16[4,16,128]{2,1,0:T(8,128)(2,1)} %q_ref.1, bf16[8192,128]{1,0:T(8,128)(2,1)} %bitcast.4, bf16[8192,128]{1,0:T(8,128)(2,1)} %bitcast.5, bf16[8192,128]{1,0:T(8,128)(2,1)} %bitcast.6, bf16[8192,128]{1,0:T(8,128)(2,1)} %bitcast.7), custom_call_target="tpu_custom_call" | custom-call | flops 8999999488 | bytes 9437184 | tf_op jit(solution)/shard_map/pallas_call | solution.py:366
  44.8 1.3 %copy.8 = bf16[4,16,128]{2,1,0:T(8,128)(2,1)} copy(bf16[4,16,128]{2,1,0:T(8,128)(2,1)} %shard_map.64) | data formatting | bytes 32768

commit v6 on v5

--- a/solution.py
+++ b/solution.py
@@ -154,11 +154,13 @@
     relay_copy(0, FAR).start()
     for dx in (3, 1, 2):
         x_copy(dx, FAR).start()
-    for dz in (7, 1, 2):
-        z_copy(Z - dz).wait_recv()
-    for dx in (2, 3, 1):
-        x_copy(dx, NEAR).start()
-    relay_copy(0, NEAR).start()
+    def pass_on_near():
+        for dz in (7, 1, 2):
+            z_copy(Z - dz).wait_recv()
+        for dx in (2, 3, 1):
+            x_copy(dx, NEAR).start()
+        relay_copy(0, NEAR).start()
+
 
     loads[1].wait()
     loop(0, GROUPS * KEYS // step, split_values)
@@ -305,6 +307,7 @@
         def _():
             merge_x(FAR)
 
+        pl.when(i == 0)(pass_on_near)
         relay_copy(dx, half).wait_recv()
         phase((queries(0, i + 1), 0, s_a, c_a), (i, 1, s_b, c_b))
 

time: 46.4 us -> 45.9 us (0.989)
  Pallas kernels: 44.8 us -> 44.3 us
    pallas_call x1, Pallas kernels: 44.8 us -> 44.3 us  [on_device(): pl.pallas_call(kernel, out_shape=jax.ShapeDtypeStruct(queries.shape, bf16...]
where the time goes in v6:
time: 45.9 us; the launch traced here: 45.6 us
  Pallas kernels  44.3 us (97%)
  local copies, waits for them, and re-layouts  1.32 us (3%)
    pallas_call x1, Pallas kernels, on_device(): pl.pallas_call(kernel, out_shape=jax.ShapeDtypeStruct(queries.shape, bf16...  44.3 us
    unnamed x1, local copies, waits for them, and re-layouts  1.32 us

profile of v6, /device:TPU:16, one launch (start us, length us, event | category | flops | bytes accessed | tf_op | source)
XLA Modules:
  0.0 45.6 jit_solution(1449967396827887800)
XLA Ops:
  0.0 44.3 %shard_map.64 = bf16[4,16,128]{2,1,0:T(8,128)(2,1)} custom-call(s32[4]{0:T(128)} %lens.1, bf16[4,16,128]{2,1,0:T(8,128)(2,1)} %q_ref.1, bf16[8192,128]{1,0:T(8,128)(2,1)} %bitcast.4, bf16[8192,128]{1,0:T(8,128)(2,1)} %bitcast.5, bf16[8192,128]{1,0:T(8,128)(2,1)} %bitcast.6, bf16[8192,128]{1,0:T(8,128)(2,1)} %bitcast.7), custom_call_target="tpu_custom_call" | custom-call | flops 8999999488 | bytes 9437184 | tf_op jit(solution)/shard_map/pallas_call | solution.py:369
  44.3 1.3 %copy.8 = bf16[4,16,128]{2,1,0:T(8,128)(2,1)} copy(bf16[4,16,128]{2,1,0:T(8,128)(2,1)} %shard_map.64) | data formatting | bytes 32768
